TPU v7x, 32 devices: a whole 2x2x4 slice. The times are simulated.
32 devices in a mesh: seq: 16 (over z, x, core), chan: 2 (over y).
Axes of the slice: x: 2, y: 2, z: 4, core: 2. Of those that a mesh axis runs over, the one named last changes fastest.
Arguments:
- signal: bfloat16 [2, 8192, 128], P('chan', 'seq'), may hold values from -6 to 6
- cotangent: bfloat16 [2, 8192, 128], P('chan', 'seq'), may hold values from -6 to 6
- band_freq: int32 [16], replicated, may hold values from 1 to 2047
- w_embed: float32 [32, 64], replicated, may hold values from -2 to 2
- b_embed: float32 [64], replicated, may hold values from -3.140625 to 3.140625
- w_out: float32 [64, 128], P(None, 'chan'), may hold values from -0.75 to 0.75
- decay: float32 [128], P('chan'), may hold values from 0.25 to 16, as said below
Outputs:
- conv_out: bfloat16 [2, 8192, 128], P('chan', 'seq')
- d_signal: bfloat16 [2, 8192, 128], P('chan', 'seq')
- grad_embed: float32 [32, 64], replicated
- grad_bias: float32 [64], replicated
- grad_out: float32 [64, 128], P(None, 'chan')
Inputs may be any that keep to these rules, and one draw needn't show every extreme that they name: decay rates are positive.
All inputs are finite; a program needn't handle non-finite values.
Results may differ from a plain program's by a relative error of at most 0.007.
Values may be sent and summed in bfloat16 or wider, within the bound.
A program may use at most 192 MiB of HBM per device.

v0:
```python
import math

import jax
import jax.numpy as jnp
from jax import lax
from jax.sharding import PartitionSpec as P

exact_mode = lax.Precision.HIGHEST


def mat_dot(lhs_mat, rhs_mat):
    return jnp.dot(lhs_mat, rhs_mat, preferred_element_type=jnp.float32, precision=exact_mode)


def side_dot(table, values):
    return jnp.einsum(
        "db,cbm->cdm", table, values, preferred_element_type=jnp.float32, precision=exact_mode
    )


def inner_dot(table, values):
    return jnp.einsum(
        "eb,cdbh->cdeh", table, values, preferred_element_type=jnp.float32, precision=exact_mode
    )


def band_phase(band_freq, places, seq_total):
    upper_part = places // 1024
    lower_part = places % 1024
    partial_turn = upper_part[:, None] * band_freq[None, :] % seq_total
    wrapped = (partial_turn * 1024 + lower_part[:, None] * band_freq[None, :]) % seq_total
    return wrapped.astype(jnp.float32) * (2.0 * math.pi / seq_total)


def filter_parts(places, band_freq, w_embed, b_embed, w_out, decay, seq_total):
    phases = band_phase(band_freq, places, seq_total)
    features = jnp.concatenate([jnp.cos(phases), jnp.sin(phases)], axis=1)
    preact = mat_dot(features, w_embed) + b_embed[None, :]
    hidden = jnp.sin(preact)
    fraction = places.astype(jnp.float32) / seq_total
    envelope = (
        jnp.exp(-decay[None, :] * fraction[:, None]) * jnp.sqrt((1.0 + decay) / seq_total)[None, :]
    )
    taps = mat_dot(hidden, w_out) * envelope
    return (features, preact, hidden, taps, envelope)


def angle_table(rows_idx, cols_idx, modulus):
    wrapped = rows_idx[:, None] * cols_idx[None, :] % modulus
    angles = wrapped.astype(jnp.float32) * (2.0 * math.pi / modulus)
    return (jnp.cos(angles), jnp.sin(angles))


def local(signal, cotangent, band_freq, w_embed, b_embed, w_out, decay):
    devices = lax.axis_size("seq")
    rank_seq = lax.axis_index("seq")
    seg_len = signal.shape[1] * 2
    channels = signal.shape[2] // 2
    block_w = seg_len // devices
    rows_all = 2 * devices
    seq_total = seg_len * devices
    fft_size = 2 * seq_total
    inv_scale = 1.0 / fft_size
    radix_one = max(
        (divisor for divisor in range(1, math.isqrt(seg_len) + 1) if seg_len % divisor == 0)
    )
    radix_two = seg_len // radix_one
    row_ids = jnp.arange(rows_all, dtype=jnp.int32)
    src_ids = jnp.arange(devices, dtype=jnp.int32)
    col_glob = rank_seq * block_w + jnp.arange(block_w, dtype=jnp.int32)
    seg_ids = jnp.arange(seg_len, dtype=jnp.int32)
    one_ids = jnp.arange(radix_one, dtype=jnp.int32)
    two_ids = jnp.arange(radix_two, dtype=jnp.int32)
    pair_ids = lax.dynamic_slice_in_dim(row_ids, 2 * rank_seq, 2)
    outer_cos, outer_sin = angle_table(row_ids, src_ids, rows_all)
    entry_cos, entry_sin = angle_table(row_ids, col_glob, fft_size)
    first_cos, first_sin = angle_table(one_ids, one_ids, radix_one)
    second_cos, second_sin = angle_table(two_ids, two_ids, radix_two)
    inner_cos, inner_sin = angle_table(one_ids, two_ids, seg_len)
    exit_cos, exit_sin = angle_table(pair_ids, seg_ids, fft_size)
    inner_c = inner_cos[None, :, :, None]
    inner_s = inner_sin[None, :, :, None]

    def twist_stack(real_a, imag_a):
        real_a = real_a.reshape(rows_all, block_w, channels)
        imag_a = imag_a.reshape(rows_all, block_w, channels)
        twist_c = entry_cos[:, :, None]
        twist_s = entry_sin[:, :, None]
        real_b = real_a * twist_c + imag_a * twist_s
        imag_b = imag_a * twist_c - real_a * twist_s
        return jnp.stack([real_b, imag_b]).reshape(2, rows_all, block_w * channels)

    def column_pass(cols_data):
        return twist_stack(mat_dot(outer_cos, cols_data), -mat_dot(outer_sin, cols_data))

    def local_forward(stacked):
        grid = stacked.reshape(2, 2, radix_one, radix_two * channels)
        part_r = side_dot(first_cos, grid[0]) + side_dot(first_sin, grid[1])
        part_i = side_dot(first_cos, grid[1]) - side_dot(first_sin, grid[0])
        part_r = part_r.reshape(2, radix_one, radix_two, channels)
        part_i = part_i.reshape(2, radix_one, radix_two, channels)
        turn_r = part_r * inner_c + part_i * inner_s
        turn_i = part_i * inner_c - part_r * inner_s
        spec_r = inner_dot(second_cos, turn_r) + inner_dot(second_sin, turn_i)
        spec_i = inner_dot(second_cos, turn_i) - inner_dot(second_sin, turn_r)
        return (spec_r, spec_i)

    def local_inverse(spec_r, spec_i):
        back_r = inner_dot(second_cos, spec_r) - inner_dot(second_sin, spec_i)
        back_i = inner_dot(second_cos, spec_i) + inner_dot(second_sin, spec_r)
        turn_r = (back_r * inner_c - back_i * inner_s).reshape(2, radix_one, radix_two * channels)
        turn_i = (back_r * inner_s + back_i * inner_c).reshape(2, radix_one, radix_two * channels)
        time_r = (side_dot(first_cos, turn_r) - side_dot(first_sin, turn_i)).reshape(
            2, seg_len, channels
        )
        time_i = (side_dot(first_cos, turn_i) + side_dot(first_sin, turn_r)).reshape(
            2, seg_len, channels
        )
        twist_c = exit_cos[:, :, None]
        twist_s = exit_sin[:, :, None]
        final_r = time_r * twist_c - time_i * twist_s
        final_i = time_r * twist_s + time_i * twist_c
        return jnp.stack([final_r, final_i]).reshape(2, 2, seg_len * channels)

    def real_rows(gathered):
        return mat_dot(outer_cos.T, gathered[0]) - mat_dot(outer_sin.T, gathered[1])

    sig_cols, cot_cols = (
        lax.all_to_all(
            signal.reshape(devices, block_w * channels),
            "seq",
            split_axis=0,
            concat_axis=0,
            tiled=True,
        ),
        lax.all_to_all(
            cotangent.reshape(devices, block_w * channels),
            "seq",
            split_axis=0,
            concat_axis=0,
            tiled=True,
        ),
    )
    places = rank_seq * seg_len + seg_ids
    features, preact, hidden, taps, envelope = filter_parts(
        places, band_freq, w_embed, b_embed, w_out, decay, seq_total
    )
    tap_cols = lax.all_to_all(
        taps.reshape(devices, block_w * channels), "seq", split_axis=0, concat_axis=0, tiled=True
    )
    spec_sig, spec_cot, spec_tap = (
        lax.all_to_all(
            column_pass(sig_cols.astype(jnp.float32)),
            "seq",
            split_axis=1,
            concat_axis=2,
            tiled=True,
        ),
        lax.all_to_all(
            column_pass(cot_cols.astype(jnp.float32)),
            "seq",
            split_axis=1,
            concat_axis=2,
            tiled=True,
        ),
        lax.all_to_all(column_pass(tap_cols), "seq", split_axis=1, concat_axis=2, tiled=True),
    )
    sig_r, sig_i = local_forward(spec_sig)
    cot_r, cot_i = local_forward(spec_cot)
    tap_r, tap_i = local_forward(spec_tap)
    prod_r = sig_r * tap_r - sig_i * tap_i
    prod_i = sig_r * tap_i + sig_i * tap_r
    grad_r = cot_r * tap_r + cot_i * tap_i
    grad_i = cot_i * tap_r - cot_r * tap_i
    corr_r = cot_r * sig_r + cot_i * sig_i
    corr_i = cot_i * sig_r - cot_r * sig_i
    prod_back, grad_back, corr_back = (
        lax.all_to_all(
            local_inverse(prod_r, prod_i), "seq", split_axis=2, concat_axis=1, tiled=True
        ),
        lax.all_to_all(
            local_inverse(grad_r, grad_i), "seq", split_axis=2, concat_axis=1, tiled=True
        ),
        lax.all_to_all(
            local_inverse(corr_r, corr_i), "seq", split_axis=2, concat_axis=1, tiled=True
        ),
    )
    out_cols = real_rows(prod_back)
    dsig_cols = real_rows(grad_back)
    dtap_cols = real_rows(corr_back) * inv_scale
    out_rows, dsig_rows = (
        lax.all_to_all(
            (out_cols * inv_scale).astype(jnp.bfloat16),
            "seq",
            split_axis=0,
            concat_axis=0,
            tiled=True,
        ),
        lax.all_to_all(
            (dsig_cols * inv_scale).astype(jnp.bfloat16),
            "seq",
            split_axis=0,
            concat_axis=0,
            tiled=True,
        ),
    )
    conv_out = out_rows.reshape(1, seg_len // 2, 2 * channels)
    d_signal = dsig_rows.reshape(1, seg_len // 2, 2 * channels)
    d_taps = (
        lax.all_to_all(
            dtap_cols.astype(jnp.bfloat16), "seq", split_axis=0, concat_axis=0, tiled=True
        )
        .astype(dtap_cols.dtype)
        .reshape(seg_len, channels)
    )
    d_raw = d_taps * envelope
    d_preact = mat_dot(d_raw, w_out.T) * jnp.cos(preact)
    out_part = mat_dot(hidden.T, d_raw)
    embed_part = mat_dot(features.T, d_preact)
    bias_part = jnp.sum(d_preact, axis=0)
    out_sum, embed_sum, bias_sum = lax.psum((out_part, embed_part, bias_part), "seq")
    embed_all, bias_all = lax.psum((embed_sum, bias_sum), "chan")
    norm_scale = 1.0 / math.sqrt(seq_total)
    return (conv_out, d_signal, embed_all * norm_scale, bias_all * norm_scale, out_sum * norm_scale)


def solution(mesh):
    return jax.shard_map(
        local,
        mesh=mesh,
        in_specs=(
            P("chan", "seq", None),
            P("chan", "seq", None),
            P(),
            P(),
            P(),
            P(None, "chan"),
            P("chan"),
        ),
        out_specs=(P("chan", "seq", None), P("chan", "seq", None), P(), P(), P(None, "chan")),
        check_vma=False,
    )
```

profile of v0, /device:TPU:0, one launch (start us, length us, event | category | flops | bytes accessed | tf_op | source)
XLA Modules:
  0.0 1505.5 jit_solution(11907168069712104977)
XLA Ops:
  4.5 7.4 all-to-all-start.6
  20.2 6.0 all-to-all-start
  98.9 6.1 all-to-all-start.3
  116.0 12.0 all-to-all-done.3
  127.9 7.1 all-to-all-start.1
  259.3 57.9 %copy.96 = f32[2,2,65536]{1,0,2:T(2,128)} copy(f32[2,2,65536]{2,1,0:T(2,128)S(1)} %pad_maximum_fusion.2) | data formatting | bytes 2097152 | tf_op jit(solution)/shard_map/stack | solution.py:123
  317.2 103.8 %reshape.642 = f32[16,1,16384]{2,1,0:T(1,128)} reshape(f32[65536,2,2]{2,1,0:T(2,128)} %bitcast.246) | data formatting | bytes 2097152
  421.0 6.0 all-to-all-start.4
  427.4 57.9 %copy.108 = f32[2,2,65536]{1,0,2:T(2,128)} copy(f32[2,2,65536]{2,1,0:T(2,128)S(1)} %pad_maximum_fusion.4) | data formatting | bytes 2097152 | tf_op jit(solution)/shard_map/stack | solution.py:123
  485.3 103.8 %reshape.648 = f32[16,1,16384]{2,1,0:T(1,128)} reshape(f32[65536,2,2]{2,1,0:T(2,128)} %bitcast.248) | data formatting | bytes 2097152
  589.1 6.2 all-to-all-start.8
  597.0 57.9 %copy.111 = f32[2,2,65536]{1,0,2:T(2,128)} copy(f32[2,2,65536]{2,1,0:T(2,128)S(1)} %pad_maximum_fusion.5) | data formatting | bytes 2097152 | tf_op jit(solution)/shard_map/stack | solution.py:123
  654.9 103.8 %reshape.652 = f32[16,1,16384]{2,1,0:T(1,128)} reshape(f32[65536,2,2]{2,1,0:T(2,128)} %bitcast.250) | data formatting | bytes 2097152
  762.4 129.0 %reshape.643 = f32[65536,2,2]{2,1,0:T(2,128)} reshape(f32[16,16384]{1,0:T(8,128)S(1)} %reduce.6) | data formatting | bytes 2097152
  891.3 75.2 %copy.97 = f32[2,2,16,4096]{3,1,2,0:T(2,128)S(1)} copy(f32[2,2,16,4096]{1,0,3,2:T(2,128)} %bitcast.27) | data formatting | bytes 2097152 | tf_op jit(solution)/shard_map/all_to_all | solution.py:178
  966.6 6.5 all-to-all-start.10
  982.4 128.6 %reshape.649 = f32[65536,2,2]{2,1,0:T(2,128)} reshape(f32[16,16384]{1,0:T(8,128)S(1)} %reduce.8) | data formatting | bytes 2097152
  1111.0 75.2 %copy.109 = f32[2,2,16,4096]{3,1,2,0:T(2,128)S(1)} copy(f32[2,2,16,4096]{1,0,3,2:T(2,128)} %bitcast.42) | data formatting | bytes 2097152 | tf_op jit(solution)/shard_map/all_to_all | solution.py:181
  1188.7 6.6 all-to-all-start.5
  1198.6 128.6 %reshape.653 = f32[65536,2,2]{2,1,0:T(2,128)} reshape(f32[16,16384]{1,0:T(8,128)S(1)} %reduce.10) | data formatting | bytes 2097152
  1327.1 75.5 %copy.112 = f32[2,2,16,4096]{3,1,2,0:T(2,128)S(1)} copy(f32[2,2,16,4096]{1,0,3,2:T(2,128)} %bitcast.51) | data formatting | bytes 2097152 | tf_op jit(solution)/shard_map/all_to_all | solution.py:184
  1405.8 6.1 all-to-all-start.9
  1436.5 58.5 %all-reduce = (f32[32,64]{1,0:T(8,128)S(1)}, f32[64]{0:T(128)S(1)}, f32[64,64]{1,0:T(8,128)S(1)}) all-reduce(f32[32,64]{1,0:T(8,128)S(1)} %fusion.65, f32[64]{0:T(128)S(1)} %get-tuple-element.72, f32[64,64]{1,0:T(8,128)S(1)} %fusion.54), channel_id=1, replica_groups=mesh['seq'=16,'chan'=2] {'seq'}, use_global_device_ids=true, to_apply=%region_0.1 | all-reduce | flops 6208 | bytes 49664 | tf_op jit(solution)/shard_map/psum | solution.py:221
  1495.0 8.3 all-reduce.1
  (234 shorter events, 269.5 us)
Async XLA Ops:
  0.6 19.2 %copy-start = (f32[64,64]{1,0:T(8,128)S(1)}, f32[64,64]{1,0:T(8,128)}, u32[]{:S(2)}) copy-start(f32[64,64]{1,0:T(8,128)} %param.12) | copy-start | bytes 49156
  4.5 15.7 %all-to-all-start.6 = ((bf16[16,2,2048]{2,1,0:T(2,128)(2,1)}), bf16[16,2,2048]{2,1,0:T(2,128)(2,1)S(1)}, u32[]{:S(2)}, u32[]{:S(2)}) async-start(bf16[16,2,2048]{2,1,0:T(2,128)(2,1)} %reshape.646), calls=%async_computation.6 | async-start | bytes 262144 | tf_op jit(solution)/shard_map/all_to_all | solution.py:136
  11.9 14.4 copy-start.11
  12.6 13.7 copy-start.15
  16.3 24.3 %copy-start.3 = (f32[1024,64]{0,1:T(8,128)}, f32[1024,64]{0,1:T(8,128)S(1)}, u32[]{:S(2)}) copy-start(f32[1024,64]{0,1:T(8,128)S(1)} %get-tuple-element.70) | copy-start | bytes 786436
  20.2 14.0 all-to-all-start
  34.2 13.7 all-to-all-start.2
  65.4 33.6 %all-to-all-start.7 = ((f32[2,32,4096]{2,0,1:T(2,128)}), f32[2,32,4096]{2,0,1:T(2,128)S(1)}, u32[]{:S(2)}, u32[]{:S(2)}) async-start(f32[2,32,4096]{2,0,1:T(2,128)} %copy.105), calls=%async_computation.7 | async-start | bytes 2097152 | tf_op jit(solution)/shard_map/all_to_all | solution.py:159
  98.9 29.0 %all-to-all-start.3 = ((f32[2,32,4096]{2,0,1:T(2,128)}), f32[2,32,4096]{2,0,1:T(2,128)S(1)}, u32[]{:S(2)}, u32[]{:S(2)}) async-start(f32[2,32,4096]{2,0,1:T(2,128)} %copy.93), calls=%async_computation.3 | async-start | bytes 2097152 | tf_op jit(solution)/shard_map/all_to_all | solution.py:166
  127.9 34.5 %all-to-all-start.1 = ((f32[2,32,4096]{2,0,1:T(2,128)}), f32[2,32,4096]{2,0,1:T(2,128)}, u32[]{:S(2)}, u32[]{:S(2)}) async-start(f32[2,32,4096]{2,0,1:T(2,128)} %copy.83), calls=%async_computation.1 | async-start | bytes 2097152 | tf_op jit(solution)/shard_map/all_to_all | solution.py:152
  259.3 167.7 %copy-start.5 = (f32[1,2,65536]{2,1,0:T(2,128)S(1)}, f32[1,2,65536]{2,1,0:T(2,128)}, u32[]{:S(2)}) copy-start(f32[1,2,65536]{2,1,0:T(2,128)} %get-tuple-element.40) | copy-start | bytes 1572868
  259.3 167.7 %copy-start.6 = (f32[1,2,65536]{2,1,0:T(2,128)S(1)}, f32[1,2,65536]{2,1,0:T(2,128)}, u32[]{:S(2)}) copy-start(f32[1,2,65536]{2,1,0:T(2,128)} %get-tuple-element.41) | copy-start | bytes 1572868
  421.0 168.1 %all-to-all-start.4 = ((f32[16,1,16384]{2,1,0:T(1,128)}), f32[16,1,16384]{2,1,0:T(1,128)S(1)}, u32[]{:S(2)}, u32[]{:S(2)}) async-start(f32[16,1,16384]{2,1,0:T(1,128)} %reshape.642), calls=%async_computation.4 | async-start | bytes 2097152 | tf_op jit(solution)/shard_map/all_to_all | solution.py:178
  589.1 377.5 %all-to-all-start.8 = ((f32[16,1,16384]{2,1,0:T(1,128)}), f32[16,1,16384]{2,1,0:T(1,128)S(1)}, u32[]{:S(2)}, u32[]{:S(2)}) async-start(f32[16,1,16384]{2,1,0:T(1,128)} %reshape.648), calls=%async_computation.8 | async-start | bytes 2097152 | tf_op jit(solution)/shard_map/all_to_all | solution.py:181
  966.6 222.1 %all-to-all-start.10 = ((f32[16,1,16384]{2,1,0:T(1,128)}), f32[16,1,16384]{2,1,0:T(1,128)S(1)}, u32[]{:S(2)}, u32[]{:S(2)}) async-start(f32[16,1,16384]{2,1,0:T(1,128)} %reshape.652), calls=%async_computation.10 | async-start | bytes 2097152 | tf_op jit(solution)/shard_map/all_to_all | solution.py:184
  1188.7 217.0 %all-to-all-start.5 = ((bf16[16,2,2048]{2,1,0:T(2,128)(2,1)}), bf16[16,2,2048]{2,1,0:T(2,128)(2,1)}, u32[]{:S(2)}, u32[]{:S(2)}) async-start(bf16[16,2,2048]{2,1,0:T(2,128)(2,1)} %reshape.644), calls=%async_computation.5 | async-start | bytes 262144 | tf_op jit(solution)/shard_map/all_to_all | solution.py:192
  1198.5 204.7 %copy-start.7 = (f32[1,16,2,4096]{3,2,1,0:T(2,128)S(1)}, f32[1,16,2,4096]{3,2,1,0:T(2,128)}, u32[]{:S(2)}) copy-start(f32[1,16,2,4096]{3,2,1,0:T(2,128)} %get-tuple-element.44) | copy-start | bytes 1572868
  1198.5 234.0 %copy-start.4 = (f32[1024,64]{0,1:T(8,128)S(1)}, f32[1024,64]{0,1:T(8,128)}, u32[]{:S(2)}) copy-start(f32[1024,64]{0,1:T(8,128)} %copy-done.3) | copy-start | bytes 786436
  1198.5 234.0 %copy-start.12 = (f32[1024]{0:T(1024)S(1)}, f32[1024]{0:T(1024)}, u32[]{:S(2)}) copy-start(f32[1024]{0:T(1024)} %copy-done.11) | copy-start | bytes 12292
  1198.5 234.0 %copy-start.14 = (f32[64]{0:T(128)S(1)}, f32[64]{0:T(128)}, u32[]{:S(2)}) copy-start(f32[64]{0:T(128)} %copy-done.13) | copy-start | bytes 772
  1198.5 234.0 %copy-start.16 = (f32[64]{0:T(128)S(1)}, f32[64]{0:T(128)}, u32[]{:S(2)}) copy-start(f32[64]{0:T(128)} %copy-done.15) | copy-start | bytes 772
  1198.5 236.8 %copy-start.9 = (f32[1024,16]{0,1:T(8,128)S(1)}, f32[1024,16]{0,1:T(8,128)}, u32[]{:S(2)}) copy-start(f32[1024,16]{0,1:T(8,128)} %copy-done.8) | copy-start | bytes 196612
  1405.8 14.1 all-to-all-start.9
  1419.8 11.4 all-to-all-start.11
  (5 other events, 24.0 us)
where the time goes:
time: 1520 us; the launch traced here: 1510 us
  local copies, waits for them, and re-layouts  1200 us (79%)
  matrix products  102 us (7%)
  starting transfers between devices  69.2 us (5%)
  blocking collectives  66.7 us (4%)
  waiting for transfers between devices  31.6 us (2%)
  other arithmetic  30.3 us (2%)
    unnamed x53, local copies, waits for them, and re-layouts  704 us
    another operation x3, local copies, waits for them, and re-layouts, local_inverse(): return jnp.stack([final_r, final_i]).reshape(2, 2, seg_len * channels)  174 us
    all_to_all x2, local copies, waits for them, and re-layouts, local(): lax.all_to_all(local_inverse(prod_r, prod_i), 'seq', split_axis=2, concat...  75.7 us
    all_to_all x1, local copies, waits for them, and re-layouts, local(): lax.all_to_all(local_inverse(corr_r, corr_i), 'seq', split_axis=2, concat...  75.5 us
    all_to_all x1, local copies, waits for them, and re-layouts, local(): lax.all_to_all(local_inverse(grad_r, grad_i), 'seq', split_axis=2, concat...  75.2 us
    psum x1, blocking collectives, local(): lax.psum((out_part, embed_part, bias_part), 'seq')  58.5 us
    dot_general x24, matrix products, inner_dot(): jnp.einsum('eb,cdbh->cdeh', table, values, preferred_element_type=jnp.flo...  49.9 us
    dot_general x24, matrix products, side_dot(): jnp.einsum('db,cbm->cdm', table, values, preferred_element_type=jnp.float...  32.9 us
  transfers between devices with their start and end apart: 12, of which 5 were waited for; matrix products, arithmetic and copies ran while one was open for 70% of the time, Pallas kernels for 0%

commit v1 on v0

--- a/solution.py
+++ b/solution.py
@@ -1,8 +1,12 @@
+import functools
 import math
 
 import jax
 import jax.numpy as jnp
+import numpy as np
 from jax import lax
+from jax.experimental import pallas as pl
+from jax.experimental.pallas import tpu as pltpu
 from jax.sharding import PartitionSpec as P
 
 exact_mode = lax.Precision.HIGHEST
@@ -51,7 +55,7 @@
     return (jnp.cos(angles), jnp.sin(angles))
 
 
-def local(signal, cotangent, band_freq, w_embed, b_embed, w_out, decay):
+def local_any(signal, cotangent, band_freq, w_embed, b_embed, w_out, decay):
     devices = lax.axis_size("seq")
     rank_seq = lax.axis_index("seq")
     seg_len = signal.shape[1] * 2
@@ -224,6 +228,444 @@
     return (conv_out, d_signal, embed_all * norm_scale, bias_all * norm_scale, out_sum * norm_scale)
 
 
+WIDE = 256
+HALF = 128
+
+
+def split_np(table):
+    high = table.astype(jnp.bfloat16)
+    low = (table - high.astype(np.float64)).astype(jnp.bfloat16)
+    return np.stack([high, low])
+
+
+def const_tables(devices, own, segs):
+    blocks = devices * segs
+    total = 2 * blocks * WIDE
+    eye = np.eye(own)
+    half_f = np.arange(blocks) + 0.5
+    alpha = 2 * np.pi * half_f[:, None] * np.arange(blocks)[None, :] / (2 * blocks)
+    outer = np.concatenate([np.kron(np.cos(alpha), eye), np.kron(-np.sin(alpha), eye)])
+    lane = np.arange(WIDE)
+    places = 2 * (lane % HALF) + lane // HALF
+    theta = np.repeat(2 * np.pi * half_f[:, None] * places[None, :] / total, own, axis=0)
+    twist = np.stack([np.cos(theta), np.sin(theta)]).astype(np.float32)
+    phi = 2 * np.pi * (places[:, None] * np.arange(WIDE)[None, :] % WIDE) / WIDE
+    inner = np.block([[np.cos(phi), -np.sin(phi)], [np.sin(phi), np.cos(phi)]])
+    chans = devices * own
+    pick = np.zeros((2, devices, segs, own, segs, 2, chans), np.float32)
+    for h in range(2):
+        for r in range(devices):
+            for q in range(segs):
+                for k in range(own):
+                    pick[h, r, q, k, q, h, r * own + k] = 1.0
+    pick = pick.reshape(2, devices * segs * own, segs * 2 * chans).astype(jnp.bfloat16)
+    return split_np(outer), split_np(inner), twist, pick
+
+
+def dot_nn(lhs, rhs):
+    return lax.dot_general(lhs, rhs, (((1,), (0,)), ((), ())), preferred_element_type=jnp.float32)
+
+
+def dot_nt(lhs, rhs):
+    return lax.dot_general(lhs, rhs, (((1,), (1,)), ((), ())), preferred_element_type=jnp.float32)
+
+
+def dot_tn(lhs, rhs):
+    return lax.dot_general(lhs, rhs, (((0,), (0,)), ((), ())), preferred_element_type=jnp.float32)
+
+
+def sin_cos(quarter):
+    whole = jnp.round(quarter)
+    rest = quarter - whole
+    sq = rest * rest
+    sin_p = rest * (1.5707963268 + sq * (-0.6459640975 + sq * (0.0796926262 + sq * (-0.0046817541 + sq * 0.00016044118))))
+    cos_p = 1.0 + sq * (-1.2337005501 + sq * (0.2536695079 + sq * (-0.0208634807 + sq * (0.00091926027 - sq * 0.0000252020424))))
+    turns = whole.astype(jnp.int32)
+    odd = (turns & 1) == 1
+    sin_v = jnp.where(odd, cos_p, sin_p)
+    cos_v = jnp.where(odd, sin_p, cos_p)
+    sin_v = jnp.where((turns & 2) == 2, -sin_v, sin_v)
+    cos_v = jnp.where(((turns + 1) & 2) == 2, -cos_v, cos_v)
+    return sin_v, cos_v
+
+
+def fused_kernel(
+    devices, planes, own, segs,
+    freq_ref, sig_ref, cot_ref, pick_ref, outer_any, inner_any, twist_any,
+    wemb_ref, bias_ref, wout_ref, decay_ref,
+    conv_ref, dsig_ref, gemb_ref, gbias_ref, gcol_ref,
+    send_a, recv_a, send_b, recv_b, hid_ref, cos_ref, taps_ref, draw_ref,
+    outer_ref, inner_ref, twist_ref, wmix_ref, rot_ref, tone_ref, wrow_ref, wcol_ref,
+    gout_ref, gmix_ref, square_ref, send_c, recv_c, send_d, recv_d,
+    send_sem, recv_sem, send_sem_d, recv_sem_d, load_sem,
+):
+    bf = jnp.bfloat16
+    me = lax.axis_index("seq")
+    blocks = devices * segs
+    rows = blocks * own
+    part = segs * own
+    seq_total = blocks * WIDE
+    per = WIDE // 64
+    groups = blocks // per
+    barrier = pltpu.get_barrier_semaphore()
+
+    lane_id = lax.axis_index("chan")
+    everyone = devices * planes
+    mine = lane_id * devices + me
+
+    def greet(step, carry):
+        peer = lax.rem(mine + step, everyone)
+        pl.semaphore_signal(
+            barrier, inc=1,
+            device_id={"seq": lax.rem(peer, devices), "chan": peer // devices},
+            device_id_type=pl.DeviceIdType.MESH,
+        )
+        return carry
+
+    lax.fori_loop(1, everyone, greet, 0)
+    loads = [
+        pltpu.make_async_copy(src, dst, load_sem.at[i])
+        for i, (src, dst) in enumerate(
+            [(outer_any, outer_ref), (inner_any, inner_ref), (twist_any, twist_ref)]
+        )
+    ]
+    for load in loads:
+        load.start()
+
+    def copy_of(phase, src, dst, step):
+        peer = lax.rem(me + step, devices)
+        return pltpu.make_async_remote_copy(
+            src_ref=src.at[peer],
+            dst_ref=dst.at[me],
+            send_sem=send_sem.at[phase, step],
+            recv_sem=recv_sem.at[phase, step],
+            device_id={"seq": peer},
+            device_id_type=pl.DeviceIdType.MESH,
+        )
+
+    def start_all(phase, src, dst):
+        def body(step, carry):
+            copy_of(phase, src, dst, step).start()
+            return carry
+
+        lax.fori_loop(1, devices, body, 0)
+
+    def wait_all(phase, src, dst):
+        def body(step, carry):
+            copy_of(phase, src, dst, step).wait()
+            return carry
+
+        lax.fori_loop(1, devices, body, 0)
+
+    def pack(x_ref, at):
+        wide = jnp.concatenate([x_ref[q * HALF:(q + 1) * HALF, :] for q in range(segs)], axis=1)
+        mixed = jnp.concatenate([dot_nt(pick_ref[h], wide) for h in range(2)], axis=1)
+        send_a[:, at:at + part, :] = mixed.astype(bf).reshape(devices, part, WIDE)
+
+    pack(sig_ref, 0)
+    pack(cot_ref, part)
+    pl.semaphore_wait(barrier, everyone - 1)
+    start_all(0, send_a, recv_a)
+    recv_a[me] = send_a[me]
+
+    turn_scale = 4.0 / seq_total
+    far_lane = lax.broadcasted_iota(jnp.int32, (blocks, HALF), 1)
+    far_row = lax.broadcasted_iota(jnp.int32, (blocks, HALF), 0)
+    near_row = lax.broadcasted_iota(jnp.int32, (HALF, WIDE), 0)
+    near_lane = lax.broadcasted_iota(jnp.int32, (HALF, WIDE), 1)
+    lane_row = lax.broadcasted_iota(jnp.int32, (1, HALF), 1)
+    lane_col = lax.broadcasted_iota(jnp.int32, (HALF, 1), 0)
+    freq_row = jnp.zeros((1, HALF), jnp.int32)
+    freq_col = jnp.zeros((HALF, 1), jnp.int32)
+    for j in range(16):
+        freq_row = jnp.where((lane_row & 15) == j, freq_ref[j], freq_row)
+        freq_col = jnp.where((lane_col & 15) == j, freq_ref[j], freq_col)
+    wrapped = (far_row * WIDE * freq_row) & (seq_total - 1)
+    far_s, far_c = sin_cos(wrapped.astype(jnp.float32) * turn_scale)
+    live = far_lane < 96
+    rot_ref[0] = jnp.where(live, far_c, jnp.where(far_lane < 98, 1.0, 0.0))
+    rot_ref[1] = jnp.where(live, jnp.where((far_lane & 16) == 0, far_s, -far_s), 0.0)
+    spot = 2 * (near_lane & (HALF - 1)) + (near_lane >> 7)
+    wrapped = (spot * freq_col) & (seq_total - 1)
+    near_s, near_c = sin_cos(wrapped.astype(jnp.float32) * turn_scale)
+    tone = jnp.where((near_row & 16) == 0, near_c, near_s)
+    tone_hi = tone.astype(bf).astype(jnp.float32)
+    tone = jnp.where((near_row >= 32) & (near_row < 64), tone - tone_hi, tone_hi)
+    tone = jnp.where(near_row < 96, tone, jnp.where(near_row < 98, 1.0, 0.0))
+    tone_ref[...] = tone.astype(bf)
+    quarter_of = 2.0 / math.pi
+    two_rows = lax.broadcasted_iota(jnp.int32, (8, 64), 0) < 2
+    for side in range(2):
+        square_ref[...] = jnp.zeros_like(square_ref)
+        for rep in range(3):
+            for half in range(2):
+                at_row = rep * 32 + 16 * (half ^ side)
+                square_ref[at_row:at_row + 16, 0:64] = wemb_ref[half * 16:half * 16 + 16, :] * quarter_of
+        if side == 0:
+            square_ref[96:104, 0:64] = jnp.where(two_rows, bias_ref[...] * quarter_of, 0.0)
+        wmix_ref[side] = square_ref[...].T[0:64, :]
+    per_own = per * own
+    w_all = wout_ref[...]
+    w_hi = w_all.astype(bf)
+    w_lo = (w_all - w_hi.astype(jnp.float32)).astype(bf)
+    chans = devices * own
+    chan_at = lax.broadcasted_iota(jnp.int32, (per_own, chans), 1)
+    chan_row = lax.broadcasted_iota(jnp.int32, (per_own, chans), 0)
+    one_hot = jnp.where(chan_at == me * own + chan_row % own, 1.0, 0.0).astype(bf)
+    row_keep = lax.broadcasted_iota(jnp.int32, (per_own, WIDE), 0) // own
+    row_keep = row_keep == lax.broadcasted_iota(jnp.int32, (per_own, WIDE), 1) // 64
+    col_keep = lax.broadcasted_iota(jnp.int32, (WIDE, per_own), 1) // own
+    col_keep = col_keep == lax.broadcasted_iota(jnp.int32, (WIDE, per_own), 0) // 64
+    for side, w_part in enumerate((w_hi, w_lo)):
+        w_rep = jnp.concatenate([w_part] * per, axis=0)
+        wrow_ref[side * per_own:(side + 1) * per_own, :] = jnp.where(
+            row_keep, dot_nt(one_hot, w_rep), 0.0
+        ).astype(bf)
+        wcol_ref[side] = jnp.where(col_keep, dot_nt(w_rep, one_hot), 0.0).astype(bf)
+    rate_at = lax.broadcasted_iota(jnp.int32, (rows, chans), 1)
+    rate_row = lax.broadcasted_iota(jnp.int32, (rows, chans), 0)
+    rate = jnp.sum(
+        jnp.where(rate_at == me * own + rate_row % own, decay_ref[...], 0.0), axis=1, keepdims=True
+    )
+    peak = jnp.sqrt((1.0 + rate) / seq_total)
+
+    lanes = lax.broadcasted_iota(jnp.int32, (64, HALF), 1)
+    high_lane = (lanes < 64) | (lanes == 97)
+
+    def net_step(g, carry):
+        mixes = []
+        for b in range(per):
+            turn_c = rot_ref[0, pl.ds(g * per + b, 1), :]
+            turn_s = rot_ref[1, pl.ds(g * per + b, 1), :]
+            mix = wmix_ref[0] * turn_c + wmix_ref[1] * turn_s
+            top = mix.astype(bf).astype(jnp.float32)
+            mixes.append(jnp.where(high_lane, top, mix - top).astype(bf))
+        quarter = dot_nn(jnp.concatenate(mixes, axis=0), tone_ref[...])
+        sin_v, cos_v = sin_cos(quarter)
+        hid = sin_v.astype(bf)
+        at = pl.multiple_of(g * WIDE, WIDE)
+        hid_ref[pl.ds(at, WIDE), :] = hid
+        cos_ref[pl.ds(at, WIDE), :] = cos_v.astype(bf)
+        both = dot_nn(wrow_ref[...], hid)
+        taps_ref[pl.ds(pl.multiple_of(g * per * own, per * own), per * own), :] = (
+            both[:per * own] + both[per * own:]
+        )
+        return carry
+
+    lax.fori_loop(0, groups, net_step, 0)
+    row_at = lax.broadcasted_iota(jnp.int32, (rows, WIDE), 0) // own
+    lane_at = lax.broadcasted_iota(jnp.int32, (rows, WIDE), 1)
+    fraction = (row_at * WIDE + 2 * (lane_at % HALF) + lane_at // HALF).astype(jnp.float32) / seq_total
+    envelope = jnp.exp(-rate * fraction) * peak
+    taps = taps_ref[...] * envelope
+
+    for load in loads:
+        load.wait()
+    cos_t = twist_ref[0]
+    sin_t = twist_ref[1]
+
+    def rest_of(stage_r, stage_i):
+        return jnp.concatenate(
+            [stage_r * cos_t + stage_i * sin_t, stage_i * cos_t - stage_r * sin_t], axis=1
+        ).astype(bf)
+
+    def inner_fwd(turned):
+        spec = dot_nn(turned, inner_ref[0]) + dot_nn(turned, inner_ref[1])
+        return spec[:, :WIDE], spec[:, WIDE:]
+
+    tap_hi = taps.astype(bf)
+    tap_lo = (taps - tap_hi.astype(jnp.float32)).astype(bf)
+    st = dot_nn(outer_ref[0], tap_hi) + dot_nn(outer_ref[1], tap_hi) + dot_nn(outer_ref[0], tap_lo)
+    tap_r, tap_i = inner_fwd(rest_of(st[:rows], st[rows:]))
+
+    wait_all(0, send_a, recv_a)
+
+    def fwd(at):
+        x = recv_a[:, at:at + part, :].reshape(rows, WIDE)
+        stage = dot_nn(outer_ref[0], x) + dot_nn(outer_ref[1], x)
+        return inner_fwd(rest_of(stage[:rows], stage[rows:]))
+
+    sig_r, sig_i = fwd(0)
+    cot_r, cot_i = fwd(part)
+
+    def back(spec_r, spec_i):
+        spec = jnp.concatenate([spec_r, spec_i], axis=1).astype(bf)
+        time = dot_nt(spec, inner_ref[0]) + dot_nt(spec, inner_ref[1])
+        time_r, time_i = time[:, :WIDE], time[:, WIDE:]
+        turned = jnp.concatenate(
+            [time_r * cos_t - time_i * sin_t, time_i * cos_t + time_r * sin_t], axis=0
+        ).astype(bf)
+        return (dot_tn(outer_ref[0], turned) + dot_tn(outer_ref[1], turned)) * (1.0 / seq_total)
+
+    out = back(sig_r * tap_r - sig_i * tap_i, sig_r * tap_i + sig_i * tap_r)
+    send_b[:, 0:part, :] = out.astype(bf).reshape(devices, part, WIDE)
+    out = back(cot_r * tap_r + cot_i * tap_i, cot_i * tap_r - cot_r * tap_i)
+    send_b[:, part:2 * part, :] = out.astype(bf).reshape(devices, part, WIDE)
+    start_all(1, send_b, recv_b)
+    recv_b[me] = send_b[me]
+
+    d_taps = back(cot_r * sig_r + cot_i * sig_i, cot_i * sig_r - cot_r * sig_i)
+    draw_ref[...] = (d_taps * envelope).astype(bf)
+    gout_ref[...] = jnp.zeros_like(gout_ref)
+    gmix_ref[...] = jnp.zeros_like(gmix_ref)
+
+    def grad_step(g, carry):
+        at = pl.multiple_of(g * WIDE, WIDE)
+        d_raw = draw_ref[pl.ds(pl.multiple_of(g * per * own, per * own), per * own), :]
+        gout_ref[...] += dot_nt(d_raw, hid_ref[pl.ds(at, WIDE), :])
+        d_hid = dot_nn(wcol_ref[0], d_raw) + dot_nn(wcol_ref[1], d_raw)
+        d_pre = (d_hid * cos_ref[pl.ds(at, WIDE), :].astype(jnp.float32)).astype(bf)
+        d_mix = dot_nt(d_pre, tone_ref[...])
+        for b in range(per):
+            turn_c = rot_ref[0, pl.ds(g * per + b, 1), :]
+            turn_s = rot_ref[1, pl.ds(g * per + b, 1), :]
+            piece = d_mix[b * 64:(b + 1) * 64, :]
+            gmix_ref[0] += piece * turn_c
+            gmix_ref[1] += piece * turn_s
+        return carry
+
+    lax.fori_loop(0, groups, grad_step, 0)
+
+    mix_lane = lax.broadcasted_iota(jnp.int32, (64, HALF), 1)
+    mix_s = gmix_ref[1]
+    crossed = jnp.where(
+        mix_lane < 16, pltpu.roll(mix_s, HALF - 16, 1),
+        jnp.where(mix_lane < 32, pltpu.roll(mix_s, 16, 1), 0.0),
+    )
+    square_ref[0:64, :] = gmix_ref[0] + crossed
+    keep = jnp.where(row_keep, gout_ref[...], 0.0)
+    keep = keep[:, :HALF] + keep[:, HALF:]
+    keep = keep + pltpu.roll(keep, 64, 1)
+    square_ref[64:64 + per_own, :] = keep
+    g_own = square_ref[64:64 + own, :]
+    for b in range(1, per):
+        g_own = g_own + square_ref[64 + b * own:64 + (b + 1) * own, :]
+    for r in range(devices):
+        send_c[r, 0:own, :] = square_ref[r * own:(r + 1) * own, :]
+        send_c[r, own:2 * own, :] = g_own
+    start_all(2, send_c, recv_c)
+    recv_c[me] = send_c[me]
+    wait_all(2, send_c, recv_c)
+    summed = recv_c[0]
+    for r in range(1, devices):
+        summed = summed + recv_c[r]
+    send_d[...] = summed
+
+    def spread_of(step):
+        peer = lax.rem(mine + step, everyone)
+        return pltpu.make_async_remote_copy(
+            src_ref=send_d,
+            dst_ref=recv_d.at[mine],
+            send_sem=send_sem_d.at[step],
+            recv_sem=recv_sem_d.at[step],
+            device_id={"seq": lax.rem(peer, devices), "chan": peer // devices},
+            device_id_type=pl.DeviceIdType.MESH,
+        )
+
+    def spread_start(step, carry):
+        spread_of(step).start()
+        return carry
+
+    def spread_wait(step, carry):
+        spread_of(step).wait()
+        return carry
+
+    lax.fori_loop(1, everyone, spread_start, 0)
+    recv_d[mine] = send_d[...]
+    wait_all(1, send_b, recv_b)
+
+    def unpack(o_ref, at):
+        x = recv_b[:, at:at + part, :].reshape(rows, WIDE)
+        wide = dot_tn(x[:, :HALF], pick_ref[0]) + dot_tn(x[:, HALF:], pick_ref[1])
+        for q in range(segs):
+            o_ref[q * HALF:(q + 1) * HALF, :] = wide[:, q * HALF:(q + 1) * HALF].astype(bf)
+
+    unpack(conv_ref, 0)
+    unpack(dsig_ref, part)
+    lax.fori_loop(1, everyone, spread_wait, 0)
+    for r in range(devices):
+        total = recv_d[r]
+        for other in range(1, planes):
+            total = total + recv_d[other * devices + r]
+        square_ref[r * own:(r + 1) * own, :] = total[0:own, :]
+        square_ref[64 + r * own:64 + (r + 1) * own, :] = recv_c[r, own:2 * own, :]
+    flipped = square_ref[...].T * (1.0 / math.sqrt(seq_total))
+    gemb_ref[...] = flipped[0:32, 0:64]
+    gbias_ref[...] = flipped[96:97, 0:64]
+    gcol_ref[...] = flipped[0:64, 64:128]
+
+
+def local(signal, cotangent, band_freq, w_embed, b_embed, w_out, decay):
+    devices = lax.axis_size("seq")
+    me = lax.axis_index("seq")
+    seg_len = signal.shape[1] * 2
+    chans = signal.shape[2] // 2
+    own = chans // devices
+    if (
+        chans % devices or seg_len % WIDE or own != 4 or seg_len * devices & (seg_len * devices - 1)
+        or seg_len * devices * 2048 > 2**30
+        or w_embed.shape != (32, 64) or chans * 2 != HALF
+    ):
+        return local_any(signal, cotangent, band_freq, w_embed, b_embed, w_out, decay)
+    segs = seg_len // WIDE
+    blocks = devices * segs
+    rows = blocks * own
+    seq_total = seg_len * devices
+    bf, f32 = jnp.bfloat16, jnp.float32
+    hidden = 64
+    per = WIDE // hidden
+    planes = lax.axis_size("chan")
+    outer, inner, twist, pick = const_tables(devices, own, segs)
+    part = segs * own
+    vmem = pl.BlockSpec(memory_space=pltpu.VMEM)
+    away = pl.BlockSpec(memory_space=pl.ANY)
+    conv, dsig, g_emb, g_bias, g_out = pl.pallas_call(
+        functools.partial(fused_kernel, devices, planes, own, segs),
+        out_shape=(
+            jax.ShapeDtypeStruct(signal.shape[1:], bf),
+            jax.ShapeDtypeStruct(signal.shape[1:], bf),
+            jax.ShapeDtypeStruct((32, hidden), f32),
+            jax.ShapeDtypeStruct((1, hidden), f32),
+            jax.ShapeDtypeStruct((hidden, chans), f32),
+        ),
+        in_specs=[pl.BlockSpec(memory_space=pltpu.SMEM)] + [vmem] * 3 + [away] * 3 + [vmem] * 4,
+        out_specs=(vmem,) * 5,
+        scratch_shapes=[pltpu.VMEM((devices, 2 * part, WIDE), bf)] * 4
+        + [pltpu.VMEM((blocks * hidden, WIDE), bf)] * 2
+        + [
+            pltpu.VMEM((rows, WIDE), f32),
+            pltpu.VMEM((rows, WIDE), bf),
+            pltpu.VMEM(outer.shape, bf),
+            pltpu.VMEM(inner.shape, bf),
+            pltpu.VMEM(twist.shape, f32),
+            pltpu.VMEM((2, hidden, HALF), f32),
+            pltpu.VMEM((2, blocks, HALF), f32),
+            pltpu.VMEM((HALF, WIDE), bf),
+            pltpu.VMEM((2 * per * own, WIDE), bf),
+            pltpu.VMEM((2, WIDE, per * own), bf),
+            pltpu.VMEM((per * own, WIDE), f32),
+            pltpu.VMEM((2, hidden, HALF), f32),
+            pltpu.VMEM((HALF, HALF), f32),
+            pltpu.VMEM((devices, 2 * own, HALF), f32),
+            pltpu.VMEM((devices, 2 * own, HALF), f32),
+            pltpu.VMEM((2 * own, HALF), f32),
+            pltpu.VMEM((devices * planes, 2 * own, HALF), f32),
+            pltpu.SemaphoreType.DMA((3, devices)),
+            pltpu.SemaphoreType.DMA((3, devices)),
+            pltpu.SemaphoreType.DMA((devices * planes,)),
+            pltpu.SemaphoreType.DMA((devices * planes,)),
+            pltpu.SemaphoreType.DMA((3,)),
+        ],
+        compiler_params=pltpu.CompilerParams(
+            collective_id=0, has_side_effects=True, vmem_limit_bytes=56 * 2**20
+        ),
+    )(
+        band_freq, signal[0], cotangent[0], jnp.asarray(pick), jnp.asarray(outer),
+        jnp.asarray(inner), jnp.asarray(twist), w_embed, b_embed[None, :], w_out, decay[None, :],
+    )
+    return (conv[None], dsig[None], g_emb, g_bias[0], g_out)
+
+
 def solution(mesh):
     return jax.shard_map(
         local,

time: 1520 us -> 46.2 us (0.03)
  local copies, waits for them, and re-layouts: 1200 us -> 4.06 us
  matrix products: 102 us -> 0 us
  starting transfers between devices: 69.2 us -> 0 us
  blocking collectives: 66.7 us -> 0 us
  Pallas kernels: 0 us -> 41.2 us
  waiting for transfers between devices: 31.6 us -> 0 us
  other arithmetic: 30.3 us -> 0 us
    unnamed x53 -> x13, local copies, waits for them, and re-layouts: 704 us -> 4.06 us
    all_to_all x8 -> x0, local copies, waits for them, and re-layouts: 231 us -> none  [the longest x2 75.7 us: local(): lax.all_to_all(local_inverse(prod_r, prod_i), 'seq', split_axis=2, concat...]
    another operation x12 -> x0, local copies, waits for them, and re-layouts: 189 us -> none  [the longest x3 174 us: local_inverse(): return jnp.stack([final_r, final_i]).reshape(2, 2, seg_len * channels)]
    dot_general x65 -> x0, matrix products: 102 us -> none  [the longest x24 49.9 us: inner_dot(): jnp.einsum('eb,cdbh->cdeh', table, values, preferred_element_type=jnp.flo...]
    all_to_all x12 -> x0, starting transfers between devices: 69.2 us -> none  [the longest x1 7.36 us: local(): lax.all_to_all(cotangent.reshape(devices, block_w * channels), 'seq', spl...]
    psum x2 -> x0, blocking collectives: 66.7 us -> none  [the longest x1 58.5 us: local(): lax.psum((out_part, embed_part, bias_part), 'seq')]
    pallas_call x0 -> x1, Pallas kernels: none -> 41.2 us  [local(): pl.pallas_call(functools.partial(fused_kernel, devices, planes, own, segs...]
    reshape x23 -> x0, local copies, waits for them, and re-layouts: 33.5 us -> none  [the longest x3 6.33 us: local_forward(): part_r = part_r.reshape(2, radix_one, radix_two, channels)]
  transfers between devices with their start and end apart: 12 -> 0, of which waited for: 5 -> 0; matrix products, arithmetic and copies ran while one was open for 70% -> 0% of each run, Pallas kernels for 0% -> 0%
where the time goes in v1:
time: 46.2 us; the launch traced here: 45.9 us
  Pallas kernels  41.2 us (89%)
  local copies, waits for them, and re-layouts  4.06 us (9%)
  between operations  0.66 us (1%)
    pallas_call x1, Pallas kernels, local(): pl.pallas_call(functools.partial(fused_kernel, devices, planes, own, segs...  41.2 us
    unnamed x13, local copies, waits for them, and re-layouts  4.06 us

profile of v1, /device:TPU:0, one launch (start us, length us, event | category | flops | bytes accessed | tf_op | source)
XLA Modules:
  0.0 45.9 jit_solution(5874289799745692869)
XLA Ops:
  0.6 41.2 %shard_map.146 = (bf16[512,128]{1,0:T(8,128)(2,1)}, bf16[512,128]{1,0:T(8,128)(2,1)}, f32[32,64]{1,0:T(8,128)}, f32[1,64]{1,0:T(1,128)}, f32[64,64]{1,0:T(8,128)}) custom-call(s32[16]{0:T(128)} %freq_ref.1, bf16[512,128]{1,0:T(8,128)(2,1)} %bitcast.7, bf16[512,128]{1,0:T(8,128)(2,1)} %bitcast.8, bf16[2,256,512]{2,1,0:T(8,128)(2,1)} %constant.8.clone.pick_ref, ...), custom_call_target="tpu_custom_call" | custom-call | tf_op jit(solution)/shard_map/pallas_call | solution.py:622
  41.9 0.0 copy-start
  41.9 1.6 %copy.21 = bf16[1,512,128]{2,1,0:T(8,128)(2,1)} copy(bf16[1,512,128]{2,1,0:T(8,128)(2,1)} %bitcast.10) | data formatting | bytes 262144
  43.5 0.0 copy-done
  43.5 0.0 copy-start.2
  43.5 0.0 copy-start.3
  43.5 0.7 %copy.22 = bf16[1,512,128]{2,1,0:T(8,128)(2,1)} copy(bf16[1,512,128]{2,1,0:T(8,128)(2,1)S(1)} %bitcast.9) | data formatting | bytes 262144
  44.1 0.1 copy-done.2
  44.2 0.0 copy-start.1
  44.2 0.6 %copy.23 = f32[32,64]{1,0:T(8,128)} copy(f32[32,64]{1,0:T(8,128)S(1)} %copy-done.2) | data formatting | bytes 16384
  44.8 0.0 copy-done.3
  44.8 0.5 %copy.24 = f32[64]{0:T(128)} copy(f32[64]{0:T(128)S(1)} %bitcast.13) | data formatting | bytes 512
  45.3 0.0 copy-done.1
  45.3 0.6 %copy.25 = f32[64,64]{1,0:T(8,128)} copy(f32[64,64]{1,0:T(8,128)S(1)} %copy-done.1) | data formatting | bytes 32768
Async XLA Ops:
  41.9 1.6 %copy-start = (bf16[512,128]{1,0:T(8,128)(2,1)S(1)}, bf16[512,128]{1,0:T(8,128)(2,1)}, u32[]{:S(2)}) copy-start(bf16[512,128]{1,0:T(8,128)(2,1)} %get-tuple-element.11) | copy-start | bytes 393220
  43.5 0.7 %copy-start.2 = (f32[32,64]{1,0:T(8,128)S(1)}, f32[32,64]{1,0:T(8,128)}, u32[]{:S(2)}) copy-start(f32[32,64]{1,0:T(8,128)} %get-tuple-element.22) | copy-start | bytes 24580
  43.5 1.3 %copy-start.3 = (f32[1,64]{1,0:T(1,128)S(1)}, f32[1,64]{1,0:T(1,128)}, u32[]{:S(2)}) copy-start(f32[1,64]{1,0:T(1,128)} %get-tuple-element.13) | copy-start | bytes 772
  44.2 1.1 %copy-start.1 = (f32[64,64]{1,0:T(8,128)S(1)}, f32[64,64]{1,0:T(8,128)}, u32[]{:S(2)}) copy-start(f32[64,64]{1,0:T(8,128)} %get-tuple-element.24) | copy-start | bytes 49156

commit v2 on v1

--- a/solution.py
+++ b/solution.py
@@ -452,7 +452,7 @@
         )
         return carry
 
-    lax.fori_loop(0, groups, net_step, 0)
+    lax.fori_loop(0, groups, net_step, 0, unroll=4)
     row_at = lax.broadcasted_iota(jnp.int32, (rows, WIDE), 0) // own
     lane_at = lax.broadcasted_iota(jnp.int32, (rows, WIDE), 1)
     fraction = (row_at * WIDE + 2 * (lane_at % HALF) + lane_at // HALF).astype(jnp.float32) / seq_total
@@ -524,7 +524,7 @@
             gmix_ref[1] += piece * turn_s
         return carry
 
-    lax.fori_loop(0, groups, grad_step, 0)
+    lax.fori_loop(0, groups, grad_step, 0, unroll=4)
 
     mix_lane = lax.broadcasted_iota(jnp.int32, (64, HALF), 1)
     mix_s = gmix_ref[1]

time: 46.2 us -> 42.4 us (0.918)
  Pallas kernels: 41.2 us -> 37.4 us
    pallas_call x1, Pallas kernels: 41.2 us -> 37.4 us  [local(): pl.pallas_call(functools.partial(fused_kernel, devices, planes, own, segs...]
where the time goes in v2:
time: 42.4 us; the launch traced here: 42.1 us
  Pallas kernels  37.4 us (88%)
  local copies, waits for them, and re-layouts  4.06 us (10%)
  between operations  0.66 us (2%)
    pallas_call x1, Pallas kernels, local(): pl.pallas_call(functools.partial(fused_kernel, devices, planes, own, segs...  37.4 us
    unnamed x13, local copies, waits for them, and re-layouts  4.06 us

profile of v2, /device:TPU:0, one launch (start us, length us, event | category | flops | bytes accessed | tf_op | source)
XLA Modules:
  0.0 42.1 jit_solution(7135756586235652517)
XLA Ops:
  0.6 37.4 %shard_map.146 = (bf16[512,128]{1,0:T(8,128)(2,1)}, bf16[512,128]{1,0:T(8,128)(2,1)}, f32[32,64]{1,0:T(8,128)}, f32[1,64]{1,0:T(1,128)}, f32[64,64]{1,0:T(8,128)}) custom-call(s32[16]{0:T(128)} %freq_ref.1, bf16[512,128]{1,0:T(8,128)(2,1)} %bitcast.7, bf16[512,128]{1,0:T(8,128)(2,1)} %bitcast.8, bf16[2,256,512]{2,1,0:T(8,128)(2,1)} %constant.8.clone.pick_ref, ...), custom_call_target="tpu_custom_call" | custom-call | tf_op jit(solution)/shard_map/pallas_call | solution.py:622
  38.1 0.0 copy-start
  38.1 1.6 %copy.21 = bf16[1,512,128]{2,1,0:T(8,128)(2,1)} copy(bf16[1,512,128]{2,1,0:T(8,128)(2,1)} %bitcast.10) | data formatting | bytes 262144
  39.7 0.0 copy-done
  39.7 0.0 copy-start.2
  39.7 0.0 copy-start.3
  39.7 0.7 %copy.22 = bf16[1,512,128]{2,1,0:T(8,128)(2,1)} copy(bf16[1,512,128]{2,1,0:T(8,128)(2,1)S(1)} %bitcast.9) | data formatting | bytes 262144
  40.3 0.1 copy-done.2
  40.4 0.0 copy-start.1
  40.4 0.6 %copy.23 = f32[32,64]{1,0:T(8,128)} copy(f32[32,64]{1,0:T(8,128)S(1)} %copy-done.2) | data formatting | bytes 16384
  41.0 0.0 copy-done.3
  41.0 0.5 %copy.24 = f32[64]{0:T(128)} copy(f32[64]{0:T(128)S(1)} %bitcast.13) | data formatting | bytes 512
  41.5 0.0 copy-done.1
  41.5 0.6 %copy.25 = f32[64,64]{1,0:T(8,128)} copy(f32[64,64]{1,0:T(8,128)S(1)} %copy-done.1) | data formatting | bytes 32768
Async XLA Ops:
  38.1 1.6 %copy-start = (bf16[512,128]{1,0:T(8,128)(2,1)S(1)}, bf16[512,128]{1,0:T(8,128)(2,1)}, u32[]{:S(2)}) copy-start(bf16[512,128]{1,0:T(8,128)(2,1)} %get-tuple-element.11) | copy-start | bytes 393220
  39.7 0.7 %copy-start.2 = (f32[32,64]{1,0:T(8,128)S(1)}, f32[32,64]{1,0:T(8,128)}, u32[]{:S(2)}) copy-start(f32[32,64]{1,0:T(8,128)} %get-tuple-element.22) | copy-start | bytes 24580
  39.7 1.3 %copy-start.3 = (f32[1,64]{1,0:T(1,128)S(1)}, f32[1,64]{1,0:T(1,128)}, u32[]{:S(2)}) copy-start(f32[1,64]{1,0:T(1,128)} %get-tuple-element.13) | copy-start | bytes 772
  40.4 1.1 %copy-start.1 = (f32[64,64]{1,0:T(8,128)S(1)}, f32[64,64]{1,0:T(8,128)}, u32[]{:S(2)}) copy-start(f32[64,64]{1,0:T(8,128)} %get-tuple-element.24) | copy-start | bytes 49156

commit v3 on v2

--- a/solution.py
+++ b/solution.py
@@ -294,7 +294,7 @@
     freq_ref, sig_ref, cot_ref, pick_ref, outer_any, inner_any, twist_any,
     wemb_ref, bias_ref, wout_ref, decay_ref,
     conv_ref, dsig_ref, gemb_ref, gbias_ref, gcol_ref,
-    send_a, recv_a, send_b, recv_b, hid_ref, cos_ref, taps_ref, draw_ref,
+    send_a, recv_a, send_b, recv_b, send_e, recv_e, hid_ref, cos_ref, taps_ref, draw_ref,
     outer_ref, inner_ref, twist_ref, wmix_ref, rot_ref, tone_ref, wrow_ref, wcol_ref,
     gout_ref, gmix_ref, square_ref, send_c, recv_c, send_d, recv_d,
     send_sem, recv_sem, send_sem_d, recv_sem_d, load_sem,
@@ -498,9 +498,7 @@
         return (dot_tn(outer_ref[0], turned) + dot_tn(outer_ref[1], turned)) * (1.0 / seq_total)
 
     out = back(sig_r * tap_r - sig_i * tap_i, sig_r * tap_i + sig_i * tap_r)
-    send_b[:, 0:part, :] = out.astype(bf).reshape(devices, part, WIDE)
-    out = back(cot_r * tap_r + cot_i * tap_i, cot_i * tap_r - cot_r * tap_i)
-    send_b[:, part:2 * part, :] = out.astype(bf).reshape(devices, part, WIDE)
+    send_b[...] = out.astype(bf).reshape(devices, part, WIDE)
     start_all(1, send_b, recv_b)
     recv_b[me] = send_b[me]
 
@@ -545,6 +543,10 @@
         send_c[r, own:2 * own, :] = g_own
     start_all(2, send_c, recv_c)
     recv_c[me] = send_c[me]
+    out = back(cot_r * tap_r + cot_i * tap_i, cot_i * tap_r - cot_r * tap_i)
+    send_e[...] = out.astype(bf).reshape(devices, part, WIDE)
+    start_all(3, send_e, recv_e)
+    recv_e[me] = send_e[me]
     wait_all(2, send_c, recv_c)
     summed = recv_c[0]
     for r in range(1, devices):
@@ -574,14 +576,15 @@
     recv_d[mine] = send_d[...]
     wait_all(1, send_b, recv_b)
 
-    def unpack(o_ref, at):
-        x = recv_b[:, at:at + part, :].reshape(rows, WIDE)
+    def unpack(o_ref, x_ref):
+        x = x_ref[...].reshape(rows, WIDE)
         wide = dot_tn(x[:, :HALF], pick_ref[0]) + dot_tn(x[:, HALF:], pick_ref[1])
         for q in range(segs):
             o_ref[q * HALF:(q + 1) * HALF, :] = wide[:, q * HALF:(q + 1) * HALF].astype(bf)
 
-    unpack(conv_ref, 0)
-    unpack(dsig_ref, part)
+    unpack(conv_ref, recv_b)
+    wait_all(3, send_e, recv_e)
+    unpack(dsig_ref, recv_e)
     lax.fori_loop(1, everyone, spread_wait, 0)
     for r in range(devices):
         total = recv_d[r]
@@ -630,7 +633,8 @@
         ),
         in_specs=[pl.BlockSpec(memory_space=pltpu.SMEM)] + [vmem] * 3 + [away] * 3 + [vmem] * 4,
         out_specs=(vmem,) * 5,
-        scratch_shapes=[pltpu.VMEM((devices, 2 * part, WIDE), bf)] * 4
+        scratch_shapes=[pltpu.VMEM((devices, 2 * part, WIDE), bf)] * 2
+        + [pltpu.VMEM((devices, part, WIDE), bf)] * 4
         + [pltpu.VMEM((blocks * hidden, WIDE), bf)] * 2
         + [
             pltpu.VMEM((rows, WIDE), f32),
@@ -650,8 +654,8 @@
             pltpu.VMEM((devices, 2 * own, HALF), f32),
             pltpu.VMEM((2 * own, HALF), f32),
             pltpu.VMEM((devices * planes, 2 * own, HALF), f32),
-            pltpu.SemaphoreType.DMA((3, devices)),
-            pltpu.SemaphoreType.DMA((3, devices)),
+            pltpu.SemaphoreType.DMA((4, devices)),
+            pltpu.SemaphoreType.DMA((4, devices)),
             pltpu.SemaphoreType.DMA((devices * planes,)),
             pltpu.SemaphoreType.DMA((devices * planes,)),
             pltpu.SemaphoreType.DMA((3,)),

time: 42.4 us -> 41.7 us (0.983)
  Pallas kernels: 37.4 us -> 36.8 us
    pallas_call x1, Pallas kernels: 37.4 us -> 36.8 us  [local(): pl.pallas_call(functools.partial(fused_kernel, devices, planes, own, segs...]
where the time goes in v3:
time: 41.7 us; the launch traced here: 41.5 us
  Pallas kernels  36.8 us (88%)
  local copies, waits for them, and re-layouts  4.06 us (10%)
  between operations  0.66 us (2%)
    pallas_call x1, Pallas kernels, local(): pl.pallas_call(functools.partial(fused_kernel, devices, planes, own, segs...  36.8 us
    unnamed x13, local copies, waits for them, and re-layouts  4.06 us

profile of v3, /device:TPU:0, one launch (start us, length us, event | category | flops | bytes accessed | tf_op | source)
XLA Modules:
  0.0 41.5 jit_solution(466428085873866509)
XLA Ops:
  0.6 36.8 %shard_map.146 = (bf16[512,128]{1,0:T(8,128)(2,1)}, bf16[512,128]{1,0:T(8,128)(2,1)}, f32[32,64]{1,0:T(8,128)}, f32[1,64]{1,0:T(1,128)}, f32[64,64]{1,0:T(8,128)}) custom-call(s32[16]{0:T(128)} %freq_ref.1, bf16[512,128]{1,0:T(8,128)(2,1)} %bitcast.7, bf16[512,128]{1,0:T(8,128)(2,1)} %bitcast.8, bf16[2,256,512]{2,1,0:T(8,128)(2,1)} %constant.8.clone.pick_ref, ...), custom_call_target="tpu_custom_call" | custom-call | tf_op jit(solution)/shard_map/pallas_call | solution.py:625
  37.4 0.0 copy-start
  37.4 1.6 %copy.21 = bf16[1,512,128]{2,1,0:T(8,128)(2,1)} copy(bf16[1,512,128]{2,1,0:T(8,128)(2,1)} %bitcast.10) | data formatting | bytes 262144
  39.0 0.0 copy-done
  39.0 0.0 copy-start.2
  39.0 0.0 copy-start.3
  39.0 0.7 %copy.22 = bf16[1,512,128]{2,1,0:T(8,128)(2,1)} copy(bf16[1,512,128]{2,1,0:T(8,128)(2,1)S(1)} %bitcast.9) | data formatting | bytes 262144
  39.7 0.1 copy-done.2
  39.7 0.0 copy-start.1
  39.7 0.6 %copy.23 = f32[32,64]{1,0:T(8,128)} copy(f32[32,64]{1,0:T(8,128)S(1)} %copy-done.2) | data formatting | bytes 16384
  40.3 0.0 copy-done.3
  40.3 0.5 %copy.24 = f32[64]{0:T(128)} copy(f32[64]{0:T(128)S(1)} %bitcast.13) | data formatting | bytes 512
  40.9 0.0 copy-done.1
  40.9 0.6 %copy.25 = f32[64,64]{1,0:T(8,128)} copy(f32[64,64]{1,0:T(8,128)S(1)} %copy-done.1) | data formatting | bytes 32768
Async XLA Ops:
  37.4 1.6 %copy-start = (bf16[512,128]{1,0:T(8,128)(2,1)S(1)}, bf16[512,128]{1,0:T(8,128)(2,1)}, u32[]{:S(2)}) copy-start(bf16[512,128]{1,0:T(8,128)(2,1)} %get-tuple-element.11) | copy-start | bytes 393220
  39.0 0.7 %copy-start.2 = (f32[32,64]{1,0:T(8,128)S(1)}, f32[32,64]{1,0:T(8,128)}, u32[]{:S(2)}) copy-start(f32[32,64]{1,0:T(8,128)} %get-tuple-element.22) | copy-start | bytes 24580
  39.0 1.3 %copy-start.3 = (f32[1,64]{1,0:T(1,128)S(1)}, f32[1,64]{1,0:T(1,128)}, u32[]{:S(2)}) copy-start(f32[1,64]{1,0:T(1,128)} %get-tuple-element.13) | copy-start | bytes 772
  39.7 1.1 %copy-start.1 = (f32[64,64]{1,0:T(8,128)S(1)}, f32[64,64]{1,0:T(8,128)}, u32[]{:S(2)}) copy-start(f32[64,64]{1,0:T(8,128)} %get-tuple-element.24) | copy-start | bytes 49156
